TPU v7x, 512 devices: a whole 4x4x16 slice. The times are simulated.
512 devices in a mesh: blk: 16 (over x_hi, y, core), dom: 32 (over z, x_lo).
Axes of the slice: x: 4 (x_hi: 2, x_lo: 2; x = x_hi * 2 + x_lo), y: 4, z: 16, core: 2. Of those that a mesh axis runs over, the one named last changes fastest.
Arguments:
- features: bfloat16 [32, 8192, 256], P('dom', 'blk'), may hold values from -6 to 6
- weight: bfloat16 [256, 256], replicated, may hold values from -0.375 to 0.375
- tiles: bfloat16 [32, 16, 16, 6, 128, 128], P('dom', 'blk'), may hold values from -0.15234375 to 0.15234375
- tile_pos: int32 [32, 16, 16, 6], P('dom', 'blk'), may hold values from 0 to 15, as said below
- tile_count: int32 [32, 16, 16], P('dom', 'blk'), may hold values from 1 to 6
- send_list: int32 [32, 16, 32, 32], P('dom', 'blk'), may hold values from 0 to 511
- send_count: int32 [32, 16, 32], P('dom', 'blk'), may hold values from 0 to 32, as said below
- owner_map: int32 [32, 16, 32, 32], P('dom', 'blk'), may hold values from 0 to 511
- halo_weight: float32 [32, 16, 32, 32], P('dom', 'blk'), may hold values from 0.25 to 1
- cotangent: bfloat16 [32, 8192, 256], P('dom', 'blk'), may hold values from -6 to 6
Outputs:
- layer_out: bfloat16 [32, 8192, 256], P('dom', 'blk')
- feature_grad: bfloat16 [32, 8192, 256], P('dom', 'blk')
- weight_grad: float32 [256, 256], replicated
Inputs may be any that keep to these rules, and one draw needn't show every extreme that they name: `tile_pos`: the 6 positions of one row group in one column group are distinct. `send_count`: zero where the peer is the sender's own partition.
All inputs are finite; a program needn't handle non-finite values.
Results may differ from a plain program's by a relative error of at most 0.019.
Values may be sent and summed in bfloat16 or wider, within the bound.
A program may use at most 128 MiB of HBM per device.

v0:
```python
import jax
import jax.numpy as jnp
from jax import lax
from jax.sharding import PartitionSpec as P


def spread_rows(tile_set, positions, counts, panel, per):
    groups, slots = positions.shape
    tile = tile_set.shape[-1]
    width = panel.shape[-1]
    grid = panel.reshape(groups, per, tile, width)
    column = positions % per
    row_tile = positions // per
    picked = grid[jnp.arange(groups)[:, None], column]
    product = jnp.einsum("gtij,gtjf->gtif", tile_set, picked, preferred_element_type=jnp.float32)
    live = jnp.arange(slots)[None, :] < counts[:, None]
    select = ((row_tile[..., None] == jnp.arange(per)[None, None, :]) & live[..., None]).astype(
        jnp.float32
    )
    return jnp.einsum("gtif,gtr->rif", product, select).reshape(per * tile, width)


def spread_cols(tile_set, positions, counts, grad_rows, per):
    groups, slots = positions.shape
    tile = tile_set.shape[-1]
    width = grad_rows.shape[-1]
    grid = grad_rows.reshape(per, tile, width)
    column = positions % per
    row_tile = positions // per
    picked = grid[row_tile]
    product = jnp.einsum("gtij,gtif->gtjf", tile_set, picked, preferred_element_type=jnp.float32)
    live = jnp.arange(slots)[None, :] < counts[:, None]
    select = ((column[..., None] == jnp.arange(per)[None, None, :]) & live[..., None]).astype(
        jnp.float32
    )
    return jnp.einsum("gtjf,gtc->gcjf", product, select).reshape(groups * per * tile, width)


def on_device(
    features,
    weight,
    tiles,
    tile_pos,
    tile_count,
    send_list,
    send_count,
    owner_map,
    halo_weight,
    cotangent,
):
    feats = features[0]
    rows, width = feats.shape
    tile_set = tiles[0, 0]
    positions = tile_pos[0, 0]
    counts = tile_count[0, 0]
    tile = tile_set.shape[-1]
    per = rows // tile
    send_rows = send_list[0, 0]
    send_live = send_count[0, 0]
    owners = owner_map[0, 0]
    edge_weight = halo_weight[0, 0]
    grad_in = cotangent[0]
    slots = send_rows.shape[1]
    live = (jnp.arange(slots)[None, :] < send_live[:, None])[..., None]
    empty = jnp.zeros((rows, width), jnp.float32)
    projected = jnp.dot(feats, weight, preferred_element_type=jnp.float32).astype(jnp.bfloat16)
    part_tiles = tile_set
    part_pos = positions
    part_count = counts
    local = spread_rows(
        part_tiles, part_pos, part_count, lax.all_gather(projected, "blk", axis=0, tiled=True), per
    )
    outgoing = jnp.where(live, projected[send_rows], jnp.zeros((), jnp.bfloat16))
    incoming = lax.all_to_all(outgoing, "dom", split_axis=0, concat_axis=0, tiled=True)
    weighted = edge_weight.reshape(-1, 1) * incoming.reshape(-1, width).astype(jnp.float32)
    halo_sum = empty.at[owners.reshape(-1)].add(weighted)
    layer_out = (local + halo_sum).astype(jnp.bfloat16)
    back = (edge_weight[..., None] * grad_in[owners].astype(jnp.float32)).astype(jnp.bfloat16)
    returned = lax.all_to_all(back, "dom", split_axis=0, concat_axis=0, tiled=True)
    returned = jnp.where(live, returned, jnp.zeros((), jnp.bfloat16))
    halo_back = empty.at[send_rows.reshape(-1)].add(returned.reshape(-1, width).astype(jnp.float32))
    part_tiles = tile_set
    part_pos = positions
    part_count = counts
    local_grad = lax.psum_scatter(
        spread_cols(part_tiles, part_pos, part_count, grad_in, per).astype(jnp.bfloat16),
        "blk",
        scatter_dimension=0,
        tiled=True,
    ).astype(jnp.float32)
    proj_grad = (local_grad + halo_back).astype(jnp.bfloat16)
    feature_grad = lax.dot_general(
        proj_grad, weight, (((1,), (1,)), ((), ())), preferred_element_type=jnp.float32
    )
    feature_grad = feature_grad.astype(jnp.bfloat16)
    weight_term = lax.dot_general(
        feats, proj_grad, (((0,), (0,)), ((), ())), preferred_element_type=jnp.float32
    )
    total = lax.psum(weight_term, ("blk", "dom"))
    scale = float(lax.axis_size("blk") * lax.axis_size("dom") * rows) ** (-0.5)
    return (layer_out[None], feature_grad[None], total * scale)


def solution(mesh):
    return jax.shard_map(
        on_device,
        mesh=mesh,
        in_specs=(
            P("dom", "blk", None),
            P(),
            P("dom", "blk", None, None, None, None),
            P("dom", "blk", None, None),
            P("dom", "blk", None),
            P("dom", "blk", None, None),
            P("dom", "blk", None),
            P("dom", "blk", None, None),
            P("dom", "blk", None, None),
            P("dom", "blk", None),
        ),
        out_specs=(P("dom", "blk", None), P("dom", "blk", None), P()),
        check_vma=False,
    )
```

profile of v0, /device:TPU:1, one launch (start us, length us, event | category | flops | bytes accessed | tf_op | source)
XLA Modules:
  0.0 745.6 jit_solution(18372749111417586942)
XLA Ops:
  10.1 6.9 gather_fusion.2
  17.0 7.3 fusion.7
  24.3 11.7 %copy.29 = bf16[16,6,256,128]{2,1,3,0:T(8,128)(2,1)} copy(bf16[16,6,256,128]{3,2,1,0:T(8,128)(2,1)} %fusion.7) | data formatting | bytes 12582912 | tf_op jit(solution)/shard_map/gtij,gtif->gtjf/dot_general | solution.py:31
  36.2 5.7 fusion.4
  41.9 2.8 copy.25
  46.2 5.0 gather_fusion.3
  51.1 2.0 fusion.17
  53.2 17.1 %all-to-all-start.1 = ((bf16[32,32,256]{2,1,0:T(8,128)(2,1)}), bf16[32,32,256]{2,1,0:T(8,128)(2,1)}, u32[]{:S(2)}, u32[]{:S(2)}) async-start(bf16[32,32,256]{2,1,0:T(8,128)(2,1)} %fusion.17), calls=%async_computation.2 | async-start | bytes 1048576 | tf_op jit(solution)/shard_map/all_to_all | solution.py:79
  73.2 5.0 gather_fusion.1
  79.5 21.9 %all-to-all-done.1 = bf16[32,32,256]{2,1,0:T(8,128)(2,1)} async-done(((bf16[32,32,256]{2,1,0:T(8,128)(2,1)}), bf16[32,32,256]{2,1,0:T(8,128)(2,1)}, u32[]{:S(2)}, u32[]{:S(2)}) %all-to-all-start.1) | async-done | bytes 524320 | tf_op jit(solution)/shard_map/all_to_all | solution.py:79
  101.4 2.4 broadcast_select_fusion
  103.7 48.7 %reduce-scatter.2.cloned.1.call-done = bf16[512,256]{1,0:T(8,128)(2,1)} async-done(((bf16[8192,256]{1,0:T(8,128)(2,1)}), bf16[512,256]{1,0:T(8,128)(2,1)}) %reduce-scatter.2.cloned.1.call-update) | async-done | bytes 262160 | tf_op jit(solution)/shard_map/reduce_scatter | solution.py:85
  152.4 1.8 convert_element_type.47
  154.2 8.3 %scatter_custom_fusion.1 = f32[512,256]{1,0:T(8,128)} fusion(f32[512,256]{1,0:T(8,128)} %convert_element_type.47, s32[1024]{0:T(1024)} %bitcast.130, bf16[1024,256]{1,0:T(8,128)(2,1)} %bitcast.127), kind=kCustom, calls=%fused_computation.20 | custom fusion | flops 524288 | bytes 1048576 | tf_op jit(solution)/shard_map/scatter-add | solution.py:81
  162.5 2.1 convolution_bitcast_fusion
  166.9 12.4 %all-to-all-start = ((bf16[32,32,256]{2,1,0:T(8,128)(2,1)}), bf16[32,32,256]{2,1,0:T(8,128)(2,1)}, u32[]{:S(2)}, u32[]{:S(2)}) async-start(bf16[32,32,256]{2,1,0:T(8,128)(2,1)} %get-tuple-element.12), calls=%async_computation | async-start | bytes 1048576 | tf_op jit(solution)/shard_map/all_to_all | solution.py:74
  179.8 2.0 fusion.14
  181.8 444.9 %all-reduce.2.cloned.1.call-done = f32[256,256]{0,1:T(8,128)} async-done(((f32[256,256]{0,1:T(8,128)}), f32[256,256]{0,1:T(8,128)}) %all-reduce.2.cloned.1.call-update) | async-done | bytes 262160 | tf_op jit(solution)/shard_map/psum | solution.py:99
  628.5 70.2 %all-gather.2.cloned.1.call-done = bf16[8192,256]{1,0:T(8,128)(2,1)} async-done(((bf16[512,256]{1,0:T(8,128)(2,1)}), bf16[8192,256]{1,0:T(8,128)(2,1)}) %all-gather.2.cloned.1.call-update) | async-done | bytes 4194320 | tf_op jit(solution)/shard_map/all_gather | solution.py:71
  698.8 8.8 %gather_fusion = bf16[96,128,256]{2,1,0:T(8,128)(2,1)} fusion(bf16[16,4,128,256]{3,2,1,0:T(8,128)(2,1)} %bitcast.123, s32[96]{0:T(128)S(1)} %reshape.324), kind=kCustom, calls=%fused_computation | custom fusion | bytes 12583680 | tf_op jit(solution)/shard_map/gather | solution.py:14
  707.6 7.3 fusion.9
  714.8 9.1 %copy.27 = bf16[16,6,256,128]{2,0,1,3:T(8,128)(2,1)} copy(bf16[16,6,256,128]{3,2,1,0:T(8,128)(2,1)} %fusion.9) | data formatting | bytes 12582912 | tf_op jit(solution)/shard_map/gtij,gtjf->gtif/dot_general | solution.py:15
  723.9 3.8 fusion.11
  728.6 8.7 %scatter_custom_fusion = f32[512,256]{1,0:T(8,128)} fusion(f32[512,256]{1,0:T(8,128)} %bitcast.126, s32[1024]{0:T(1024)S(1)} %bitcast.129, bf16[1024,256]{1,0:T(8,128)(2,1)} %bitcast.31, f32[1024]{0:T(1024)S(1)} %mul.26), kind=kCustom, calls=%fused_computation.25 | custom fusion | flops 786432 | bytes 1052672 | tf_op jit(solution)/shard_map/scatter-add | solution.py:76
  (57 shorter events, 15.9 us)
Async XLA Ops:
  7.2 9.8 %copy-start = (bf16[1,1,16,6,128,128]{5,4,3,2,1,0:T(8,128)(2,1)S(1)}, bf16[1,1,16,6,128,128]{5,4,3,2,1,0:T(8,128)(2,1)}, u32[]{:S(2)}) copy-start(bf16[1,1,16,6,128,128]{5,4,3,2,1,0:T(8,128)(2,1)} %param.12) | copy-start | bytes 9437188
  7.2 145.2 %reduce-scatter.2.cloned.1.call-start = ((), (), s32[]{:S(2)}) async-start(), calls=%async_computation.4 | async-start | bytes 4456448 | tf_op jit(solution)/shard_map/reduce_scatter | solution.py:85
  24.3 11.8 %copy-start.9 = (s32[1,1,16]{2,1,0:T(1,128)S(1)}, s32[1,1,16]{2,1,0:T(1,128)}, u32[]{:S(2)}) copy-start(s32[1,1,16]{2,1,0:T(1,128)} %param.14) | copy-start | bytes 196
  36.2 5.7 copy-start.5
  41.9 2.8 copy-start.4
  41.9 4.2 copy-start.1
  44.7 27.3 %copy-start.3 = (bf16[256,256]{1,0:T(8,128)(2,1)S(1)}, bf16[256,256]{1,0:T(8,128)(2,1)}, u32[]{:S(2)}) copy-start(bf16[256,256]{1,0:T(8,128)(2,1)} %param.11) | copy-start | bytes 393220
  53.2 48.2 %all-to-all-start.1 = ((bf16[32,32,256]{2,1,0:T(8,128)(2,1)}), bf16[32,32,256]{2,1,0:T(8,128)(2,1)}, u32[]{:S(2)}, u32[]{:S(2)}) async-start(bf16[32,32,256]{2,1,0:T(8,128)(2,1)} %fusion.17), calls=%async_computation.2 | async-start | bytes 1048576 | tf_op jit(solution)/shard_map/all_to_all | solution.py:79
  70.3 109.3 %copy-start.7 = (s32[16,6]{0,1:T(8,128)S(1)}, s32[16,6]{0,1:T(8,128)}, u32[]{:S(2)}) copy-start(s32[16,6]{0,1:T(8,128)} %get-tuple-element.14) | copy-start | bytes 1156
  70.3 109.4 %copy-start.6 = (pred[16,6]{1,0:T(8,128)(4,1)S(1)}, pred[16,6]{1,0:T(8,128)(4,1)}, u32[]{:S(2)}) copy-start(pred[16,6]{1,0:T(8,128)(4,1)} %copy-done.5) | copy-start | bytes 292
  70.3 556.4 %all-reduce.2.cloned.1.call-start = ((), (), s32[]{:S(2)}) async-start(), calls=%async_computation.5 | async-start | bytes 524288 | tf_op jit(solution)/shard_map/psum | solution.py:99
  73.2 91.5 %copy-start.2 = (bf16[512,256]{1,0:T(8,128)(2,1)}, bf16[512,256]{1,0:T(8,128)(2,1)S(1)}, u32[]{:S(2)}) copy-start(bf16[512,256]{1,0:T(8,128)(2,1)S(1)} %convolution_convert_fusion.1) | copy-start | bytes 786436
  79.5 99.9 %copy-start.8 = (s32[16,6,1]{0,2,1:T(1,128)S(1)}, s32[16,6,1]{0,2,1:T(1,128)}, u32[]{:S(2)}) copy-start(s32[16,6,1]{0,2,1:T(1,128)} %get-tuple-element.10) | copy-start | bytes 1156
  164.6 534.2 %all-gather.2.cloned.1.call-start = ((), (), s32[]{:S(2)}) async-start(), calls=%async_computation.3 | async-start | bytes 4456448 | tf_op jit(solution)/shard_map/all_gather | solution.py:71
  166.9 561.7 %all-to-all-start = ((bf16[32,32,256]{2,1,0:T(8,128)(2,1)}), bf16[32,32,256]{2,1,0:T(8,128)(2,1)}, u32[]{:S(2)}, u32[]{:S(2)}) async-start(bf16[32,32,256]{2,1,0:T(8,128)(2,1)} %get-tuple-element.12), calls=%async_computation | async-start | bytes 1048576 | tf_op jit(solution)/shard_map/all_to_all | solution.py:74
Sparse Core Ops, SparseCore 0:
  44.9 107.5 reduce-scatter.1
  164.7 461.9 all-reduce.1
  630.6 68.0 all-gather.1
where the time goes:
time: 747 us; the launch traced here: 746 us
  waiting for transfers between devices  586 us (78%)
  local copies, waits for them, and re-layouts  54.8 us (7%)
  other arithmetic  31.5 us (4%)
  starting transfers between devices  29.7 us (4%)
  matrix products  29.4 us (4%)
  between operations  13.9 us (2%)
    psum x1, waiting for transfers between devices, on_device(): total = lax.psum(weight_term, ('blk', 'dom'))  445 us
    all_gather x1, waiting for transfers between devices, on_device(): lax.all_gather(projected, 'blk', axis=0, tiled=True)  70.2 us
    reduce_scatter x1, waiting for transfers between devices, on_device(): lax.psum_scatter(spread_cols(part_tiles, part_pos, part_count, grad_in, p...  48.7 us
    all_to_all x1, waiting for transfers between devices, on_device(): lax.all_to_all(back, 'dom', split_axis=0, concat_axis=0, tiled=True)  21.9 us
    all_to_all x1, starting transfers between devices, on_device(): lax.all_to_all(back, 'dom', split_axis=0, concat_axis=0, tiled=True)  17.1 us
  transfers between devices with their start and end apart: 5, of which 4 were waited for; matrix products, arithmetic and copies ran while one was open for 7% of the time, Pallas kernels for 0%

commit v1 on v0

--- a/solution.py
+++ b/solution.py
@@ -96,7 +96,9 @@
     weight_term = lax.dot_general(
         feats, proj_grad, (((0,), (0,)), ((), ())), preferred_element_type=jnp.float32
     )
-    total = lax.psum(weight_term, ("blk", "dom"))
+    total = weight_term
+    for j in ("dom", "blk"):
+        total = lax.psum(total, axis_name=j)
     scale = float(lax.axis_size("blk") * lax.axis_size("dom") * rows) ** (-0.5)
     return (layer_out[None], feature_grad[None], total * scale)
 

time: 747 us -> 707 us (0.946)
  waiting for transfers between devices: 586 us -> 549 us
    psum x1 -> x2, waiting for transfers between devices: 445 us -> 403 us  [on_device(): total = lax.psum(total, axis_name=j)]
  transfers between devices with their start and end apart: 5 -> 6, of which waited for: 4 -> 5; matrix products, arithmetic and copies ran while one was open for 7% -> 8% of each run, Pallas kernels for 0% -> 0%
where the time goes in v1:
time: 707 us; the launch traced here: 705 us
  waiting for transfers between devices  549 us (78%)
  local copies, waits for them, and re-layouts  54.8 us (8%)
  other arithmetic  31.5 us (4%)
  matrix products  29.4 us (4%)
  starting transfers between devices  26.3 us (4%)
  between operations  13.9 us (2%)
    psum x2, waiting for transfers between devices, on_device(): total = lax.psum(total, axis_name=j)  403 us
    all_gather x1, waiting for transfers between devices, on_device(): lax.all_gather(projected, 'blk', axis=0, tiled=True)  74.7 us
    reduce_scatter x1, waiting for transfers between devices, on_device(): lax.psum_scatter(spread_cols(part_tiles, part_pos, part_count, grad_in, p...  48.7 us
    all_to_all x1, waiting for transfers between devices, on_device(): lax.all_to_all(back, 'dom', split_axis=0, concat_axis=0, tiled=True)  21.9 us
    all_to_all x1, starting transfers between devices, on_device(): lax.all_to_all(back, 'dom', split_axis=0, concat_axis=0, tiled=True)  17.1 us
  transfers between devices with their start and end apart: 6, of which 5 were waited for; matrix products, arithmetic and copies ran while one was open for 8% of the time, Pallas kernels for 0%

profile of v1, /device:TPU:1, one launch (start us, length us, event | category | flops | bytes accessed | tf_op | source)
XLA Modules:
  0.0 705.1 jit_solution(15689746616510293321)
XLA Ops:
  10.1 6.9 gather_fusion.2
  17.0 7.3 %fusion.7 = bf16[16,6,256,128]{3,2,1,0:T(8,128)(2,1)} fusion(bf16[16,6,128,256]{3,2,1,0:T(8,128)(2,1)} %bitcast.121, bf16[1,1,16,6,128,128]{5,4,3,2,1,0:T(8,128)(2,1)S(1)} %copy-done), kind=kOutput, calls=%fused_computation.11 | convolution fusion | flops 805306368 | bytes 15728640 | tf_op jit(solution)/shard_map/gtij,gtif->gtjf/dot_general | solution.py:31
  24.3 11.7 %copy.29 = bf16[16,6,256,128]{2,1,3,0:T(8,128)(2,1)} copy(bf16[16,6,256,128]{3,2,1,0:T(8,128)(2,1)} %fusion.7) | data formatting | bytes 12582912 | tf_op jit(solution)/shard_map/gtij,gtif->gtjf/dot_general | solution.py:31
  36.2 5.7 fusion.4
  41.9 2.8 copy.25
  46.2 5.0 gather_fusion.3
  51.1 2.0 fusion.17
  53.2 17.1 %all-to-all-start.1 = ((bf16[32,32,256]{2,1,0:T(8,128)(2,1)}), bf16[32,32,256]{2,1,0:T(8,128)(2,1)}, u32[]{:S(2)}, u32[]{:S(2)}) async-start(bf16[32,32,256]{2,1,0:T(8,128)(2,1)} %fusion.17), calls=%async_computation.2 | async-start | bytes 1048576 | tf_op jit(solution)/shard_map/all_to_all | solution.py:79
  73.2 5.0 gather_fusion.1
  79.5 21.9 %all-to-all-done.1 = bf16[32,32,256]{2,1,0:T(8,128)(2,1)} async-done(((bf16[32,32,256]{2,1,0:T(8,128)(2,1)}), bf16[32,32,256]{2,1,0:T(8,128)(2,1)}, u32[]{:S(2)}, u32[]{:S(2)}) %all-to-all-start.1) | async-done | bytes 524320 | tf_op jit(solution)/shard_map/all_to_all | solution.py:79
  101.4 2.4 broadcast_select_fusion
  103.7 48.7 %reduce-scatter.2.cloned.1.call-done = bf16[512,256]{1,0:T(8,128)(2,1)} async-done(((bf16[8192,256]{1,0:T(8,128)(2,1)}), bf16[512,256]{1,0:T(8,128)(2,1)}) %reduce-scatter.2.cloned.1.call-update) | async-done | bytes 262160 | tf_op jit(solution)/shard_map/reduce_scatter | solution.py:85
  154.2 8.3 %scatter_custom_fusion.1 = f32[512,256]{1,0:T(8,128)} fusion(f32[512,256]{1,0:T(8,128)} %convert_element_type.47, s32[1024]{0:T(1024)} %bitcast.130, bf16[1024,256]{1,0:T(8,128)(2,1)} %bitcast.127), kind=kCustom, calls=%fused_computation.20 | custom fusion | flops 524288 | bytes 1048576 | tf_op jit(solution)/shard_map/scatter-add | solution.py:81
  162.5 2.1 convolution_bitcast_fusion
  164.6 241.2 %all-reduce.3.cloned.1.call-done = f32[256,256]{0,1:T(8,128)} async-done(((f32[256,256]{0,1:T(8,128)}), f32[256,256]{0,1:T(8,128)}) %all-reduce.3.cloned.1.call-update) | async-done | bytes 262160 | tf_op jit(solution)/shard_map/psum | solution.py:101
  408.1 9.0 %all-to-all-start = ((bf16[32,32,256]{2,1,0:T(8,128)(2,1)}), bf16[32,32,256]{2,1,0:T(8,128)(2,1)}, u32[]{:S(2)}, u32[]{:S(2)}) async-start(bf16[32,32,256]{2,1,0:T(8,128)(2,1)} %get-tuple-element.12), calls=%async_computation | async-start | bytes 1048576 | tf_op jit(solution)/shard_map/all_to_all | solution.py:74
  417.5 2.0 fusion.14
  419.5 162.2 %all-reduce.5.cloned.1.call-done = f32[256,256]{0,1:T(8,128)} async-done(((f32[256,256]{0,1:T(8,128)}), f32[256,256]{0,1:T(8,128)}) %all-reduce.5.cloned.1.call-update) | async-done | bytes 262160 | tf_op jit(solution)/shard_map/psum | solution.py:101
  583.5 74.7 %all-gather.2.cloned.1.call-done = bf16[8192,256]{1,0:T(8,128)(2,1)} async-done(((bf16[512,256]{1,0:T(8,128)(2,1)}), bf16[8192,256]{1,0:T(8,128)(2,1)}) %all-gather.2.cloned.1.call-update) | async-done | bytes 4194320 | tf_op jit(solution)/shard_map/all_gather | solution.py:71
  658.2 8.8 %gather_fusion = bf16[96,128,256]{2,1,0:T(8,128)(2,1)} fusion(bf16[16,4,128,256]{3,2,1,0:T(8,128)(2,1)} %bitcast.123, s32[96]{0:T(128)S(1)} %reshape.324), kind=kCustom, calls=%fused_computation | custom fusion | bytes 12583680 | tf_op jit(solution)/shard_map/gather | solution.py:14
  667.0 7.3 %fusion.9 = bf16[16,6,256,128]{3,2,1,0:T(8,128)(2,1)} fusion(bf16[16,6,128,256]{3,2,1,0:T(8,128)(2,1)} %bitcast.120, bf16[1,1,16,6,128,128]{5,4,3,2,1,0:T(8,128)(2,1)S(1)} %copy-done), kind=kOutput, calls=%fused_computation.13 | convolution fusion | flops 805306368 | bytes 15728640 | tf_op jit(solution)/shard_map/gtij,gtjf->gtif/dot_general | solution.py:15
  674.3 9.1 %copy.27 = bf16[16,6,256,128]{2,0,1,3:T(8,128)(2,1)} copy(bf16[16,6,256,128]{3,2,1,0:T(8,128)(2,1)} %fusion.9) | data formatting | bytes 12582912 | tf_op jit(solution)/shard_map/gtij,gtjf->gtif/dot_general | solution.py:15
  683.4 3.8 fusion.11
  688.1 8.7 %scatter_custom_fusion = f32[512,256]{1,0:T(8,128)} fusion(f32[512,256]{1,0:T(8,128)} %bitcast.126, s32[1024]{0:T(1024)S(1)} %bitcast.129, bf16[1024,256]{1,0:T(8,128)(2,1)} %bitcast.31, f32[1024]{0:T(1024)S(1)} %mul.26), kind=kCustom, calls=%fused_computation.25 | custom fusion | flops 786432 | bytes 1052672 | tf_op jit(solution)/shard_map/scatter-add | solution.py:76
  (60 shorter events, 17.6 us)
Async XLA Ops:
  7.2 9.8 %copy-start = (bf16[1,1,16,6,128,128]{5,4,3,2,1,0:T(8,128)(2,1)S(1)}, bf16[1,1,16,6,128,128]{5,4,3,2,1,0:T(8,128)(2,1)}, u32[]{:S(2)}) copy-start(bf16[1,1,16,6,128,128]{5,4,3,2,1,0:T(8,128)(2,1)} %param.12) | copy-start | bytes 9437188
  7.2 145.2 %reduce-scatter.2.cloned.1.call-start = ((), (), s32[]{:S(2)}) async-start(), calls=%async_computation.4 | async-start | bytes 4456448 | tf_op jit(solution)/shard_map/reduce_scatter | solution.py:85
  24.3 11.8 %copy-start.9 = (s32[1,1,16]{2,1,0:T(1,128)S(1)}, s32[1,1,16]{2,1,0:T(1,128)}, u32[]{:S(2)}) copy-start(s32[1,1,16]{2,1,0:T(1,128)} %param.14) | copy-start | bytes 196
  36.2 5.7 copy-start.5
  41.9 2.8 copy-start.4
  41.9 4.2 copy-start.1
  44.7 27.3 %copy-start.3 = (bf16[256,256]{1,0:T(8,128)(2,1)S(1)}, bf16[256,256]{1,0:T(8,128)(2,1)}, u32[]{:S(2)}) copy-start(bf16[256,256]{1,0:T(8,128)(2,1)} %param.11) | copy-start | bytes 393220
  53.2 48.2 %all-to-all-start.1 = ((bf16[32,32,256]{2,1,0:T(8,128)(2,1)}), bf16[32,32,256]{2,1,0:T(8,128)(2,1)}, u32[]{:S(2)}, u32[]{:S(2)}) async-start(bf16[32,32,256]{2,1,0:T(8,128)(2,1)} %fusion.17), calls=%async_computation.2 | async-start | bytes 1048576 | tf_op jit(solution)/shard_map/all_to_all | solution.py:79
  70.3 347.0 %copy-start.7 = (s32[16,6]{0,1:T(8,128)S(1)}, s32[16,6]{0,1:T(8,128)}, u32[]{:S(2)}) copy-start(s32[16,6]{0,1:T(8,128)} %get-tuple-element.14) | copy-start | bytes 1156
  70.3 347.1 %copy-start.6 = (pred[16,6]{1,0:T(8,128)(4,1)S(1)}, pred[16,6]{1,0:T(8,128)(4,1)}, u32[]{:S(2)}) copy-start(pred[16,6]{1,0:T(8,128)(4,1)} %copy-done.5) | copy-start | bytes 292
  70.3 335.6 %all-reduce.3.cloned.1.call-start = ((), (), s32[]{:S(2)}) async-start(), calls=%async_computation.5 | async-start | bytes 524288 | tf_op jit(solution)/shard_map/psum | solution.py:101
  73.2 332.8 %copy-start.2 = (bf16[512,256]{1,0:T(8,128)(2,1)}, bf16[512,256]{1,0:T(8,128)(2,1)S(1)}, u32[]{:S(2)}) copy-start(bf16[512,256]{1,0:T(8,128)(2,1)S(1)} %convolution_convert_fusion.1) | copy-start | bytes 786436
  79.5 337.6 %copy-start.8 = (s32[16,6,1]{0,2,1:T(1,128)S(1)}, s32[16,6,1]{0,2,1:T(1,128)}, u32[]{:S(2)}) copy-start(s32[16,6,1]{0,2,1:T(1,128)} %get-tuple-element.10) | copy-start | bytes 1156
  164.6 417.1 %all-reduce.5.cloned.1.call-start = ((), (), s32[]{:S(2)}) async-start(), calls=%async_computation.6 | async-start | bytes 524288 | tf_op jit(solution)/shard_map/psum | solution.py:101
  405.9 252.3 %all-gather.2.cloned.1.call-start = ((), (), s32[]{:S(2)}) async-start(), calls=%async_computation.3 | async-start | bytes 4456448 | tf_op jit(solution)/shard_map/all_gather | solution.py:71
  408.1 280.0 %all-to-all-start = ((bf16[32,32,256]{2,1,0:T(8,128)(2,1)}), bf16[32,32,256]{2,1,0:T(8,128)(2,1)}, u32[]{:S(2)}, u32[]{:S(2)}) async-start(bf16[32,32,256]{2,1,0:T(8,128)(2,1)} %get-tuple-element.12), calls=%async_computation | async-start | bytes 1048576 | tf_op jit(solution)/shard_map/all_to_all | solution.py:74
Sparse Core Ops, SparseCore 0:
  44.9 107.5 reduce-scatter.1
  164.7 241.1 all-reduce.2
  408.8 172.8 all-reduce.4
  586.0 72.1 all-gather.1
